TPU v7x, 512 devices: a whole 4x8x8 slice. The times are simulated.
512 devices in a mesh: bucket: 16 (over z_lo, x, core), edge: 32 (over z_hi, y).
Axes of the slice: x: 4, y: 8, z: 8 (z_hi: 4, z_lo: 2; z = z_hi * 2 + z_lo), core: 2. Of those that a mesh axis runs over, the one named last changes fastest.
Arguments:
- left_emb: float32 [131072, 400], P(('bucket', 'edge')), may hold values from -20 to 20
- right_emb: float32 [131072, 400], P(('bucket', 'edge')), may hold values from -20 to 20
- left_state: float32 [131072], P(('bucket', 'edge')), may hold values from 0.1 to 10
- right_state: float32 [131072], P(('bucket', 'edge')), may hold values from 0.1 to 10
- relations: float32 [1024, 400], replicated, may hold values from 0.1 to 1.9
- src_rows: int32 [16, 2, 8192], P('bucket', None, 'edge'), may hold values from 0 to 8191, as said below
- dst_rows: int32 [16, 2, 8192], P('bucket', None, 'edge'), may hold values from 0 to 8191, as said below
- rel_ids: int32 [16, 2, 8192], P('bucket', None, 'edge'), may hold values from 0 to 1023
- neg_rows: int32 [16, 2, 8192], P('bucket', None, 'edge'), may hold values from 0 to 8191, as said below
Outputs:
- left_next: float32 [131072, 400], P(('bucket', 'edge'))
- left_state_next: float32 [131072], P(('bucket', 'edge'))
- right_next: float32 [131072, 400], P(('bucket', 'edge'))
- right_state_next: float32 [131072], P(('bucket', 'edge'))
Inputs may be any that keep to these rules, and one draw needn't show every extreme that they name: `src_rows`: of the 256 sources of one bucket, sub-round and index of edge, at most 12 lie in the rows held by any one index of edge; in each bucket and sub-round one index's rows receive exactly 12 from every index. `dst_rows`: likewise for the 256 destinations of one bucket, sub-round and index of edge. `neg_rows`: likewise for the 256 negatives of one bucket, sub-round and index of edge; a block's negatives may repeat rows and may equal its edges' destinations.
All inputs are finite; a program needn't handle non-finite values.
Results may differ from a plain program's by a relative error of at most 0.0037.
Values may be sent and summed in bfloat16 or wider, within the bound.
No kernel may reach another device: no remote copies, remote signals or barrier semaphores. Data moves between devices by JAX's collectives and lax.ppermute only.
A program may use at most 64 MiB of HBM per device.

v0:
```python
import jax
import jax.numpy as jnp
from jax import lax
from jax.experimental import pallas as pl
from jax.experimental.pallas import tpu as pltpu
from jax.sharding import PartitionSpec as P

SUBS = 2
D = 400
K = 256
HOLD = 32
CAP = 12
LANE = 128
WIDE = 512
TAIL = 16
REST = 3 * LANE
SLOT_A = 32
SLOT_B = 8
ROW_A = HOLD * SLOT_A
ROWS_J = HOLD * (SLOT_A + SLOT_B)
BLOCK = 3 * (SLOT_A + SLOT_B)
STEP = 64

sharp = 40.0
rate = 0.5
tiny = 1e-06
guard = 1e-10

f32 = jnp.float32
bf16 = jnp.bfloat16
i32 = jnp.int32


def iota(shape, dim):
    return lax.broadcasted_iota(i32, shape, dim)


def mm(first, second):
    return lax.dot_general(first, second, (((1,), (0,)), ((), ())), preferred_element_type=f32)


def mm_nt(first, second):
    return lax.dot_general(first, second, (((1,), (1,)), ((), ())), preferred_element_type=f32)


def as_half(mask):
    return mask.astype(f32).astype(bf16)


def plan_kernel(src_ref, dst_ref, neg_ref, want_ref, place_ref):
    refs = (src_ref, dst_ref, neg_ref)
    lists = [refs[kind][step : step + 1, :] for step in range(SUBS) for kind in range(3)]
    holder = iota((HOLD, K), 0)
    hits = [(holder == (row >> 8)).astype(f32) for row in lists]
    upto = as_half(iota((K, K), 0) <= iota((K, K), 1))
    counts = mm(jnp.concatenate(hits, axis=0).astype(bf16), upto)
    want = jnp.zeros((HOLD, LANE), f32)
    slots = iota((LANE, K), 0)
    places = []
    for number, row in enumerate(lists):
        step, kind = divmod(number, 3)
        hit = hits[number]
        count = counts[number * HOLD : (number + 1) * HOLD, :]
        order = jnp.sum(hit * count, axis=0, keepdims=True).astype(i32) - 1
        slot = order + kind * CAP
        owner = row >> 8
        local = (row & 255).astype(f32)
        chosen = as_half(slots == slot + step * STEP)
        want = want + mm_nt((hit * local).astype(bf16), chosen)
        places.append(
            jnp.where(slot < SLOT_A, owner * SLOT_A + slot, ROW_A + owner * SLOT_B + slot - SLOT_A)
        )
    places.append(jnp.zeros((2, K), i32))
    place_ref[...] = jnp.concatenate(places, axis=0)
    slot = iota((HOLD, LANE), 1) & (STEP - 1)
    base = jnp.where(slot < CAP, 0, jnp.where(slot < 3 * CAP, K, 4 * K))
    want_ref[:, 0, :] = want.astype(i32) + base


def edge_kernel(place_ref, *out_refs):
    place = place_ref[...].astype(f32)
    tall = jnp.concatenate([place, jnp.zeros((LANE - 8, K), f32)], axis=0)
    columns = jnp.transpose(tall).astype(i32)
    for step in range(SUBS):
        to_slot, to_edge = out_refs[2 * step], out_refs[2 * step + 1]
        for kind in range(3):
            number = step * 3 + kind
            to_slot[:, kind * K : (kind + 1) * K] = as_half(
                iota((ROWS_J, K), 0) == place_ref[number : number + 1, :]
            )
            to_edge[kind * K : (kind + 1) * K, :] = as_half(
                iota((K, ROWS_J), 1) == columns[:, number : number + 1]
            )


def asked(got_ref, step):
    got = got_ref[:, 0, :].astype(f32)
    square = jnp.concatenate([got, jnp.zeros((LANE - HOLD, LANE), f32)], axis=0)
    turned = jnp.transpose(square).astype(i32)
    low = step * STEP
    parts = []
    for start, size in ((low, SLOT_A), (low + SLOT_A, SLOT_B)):
        for holder in range(HOLD):
            column = turned[start : start + size, holder : holder + 1]
            parts.append((iota((size, 2 * K), 1) == column).astype(f32))
    return jnp.concatenate(parts, axis=0)


def held_kernel(got_ref, sum_first_ref, serve_ref, sum_second_ref):
    sum_first_ref[...] = jnp.transpose(asked(got_ref, 0)).astype(bf16)
    second = asked(got_ref, 1)
    serve_ref[...] = second.astype(bf16)
    sum_second_ref[...] = jnp.transpose(second).astype(bf16)


def group_mask(shape):
    return (iota(shape, len(shape) - 1) >> 4) == iota(shape, len(shape) - 2)


def pack(values, out_ref):
    keep = group_mask((HOLD, SLOT_B, LANE))
    sub = iota((HOLD, SLOT_B, LANE), 1)
    firsts = values[:ROW_A].reshape(HOLD, SLOT_A, WIDE)
    lasts = values[ROW_A:].reshape(HOLD, SLOT_B, WIDE)
    ends = [lasts[:, :, c * LANE : (c + 1) * LANE] for c in range(3)]
    for c in range(3):
        out_ref[:, c * SLOT_A : (c + 1) * SLOT_A, :] = firsts[
            :, :, c * LANE : (c + 1) * LANE
        ].astype(bf16)
    for m in range(4):
        piece = firsts[:, m * 8 : (m + 1) * 8, REST:]
        row = jnp.sum(jnp.where(keep, piece, 0.0), axis=1, keepdims=True)
        ends[0] = jnp.where(sub == 4 + m, row, ends[0])
    row = jnp.sum(jnp.where(keep, lasts[:, :, REST:], 0.0), axis=1, keepdims=True)
    ends[1] = jnp.where(sub == 4, row, ends[1])
    out_ref[:, 3 * SLOT_A :, :] = jnp.concatenate(ends, axis=1).astype(bf16)


def unpack(in_ref):
    keep = group_mask((HOLD, SLOT_B, LANE))
    ends = in_ref[:, 3 * SLOT_A :, :].astype(f32)
    tails = []
    for m in range(5):
        at = 4 + m if m < 4 else 12
        row = ends[:, at : at + 1, :]
        tails.append(jnp.where(keep, row, 0.0))
    chunks = []
    for c in range(3):
        first = in_ref[:, c * SLOT_A : (c + 1) * SLOT_A, :].reshape(ROW_A, LANE)
        last = ends[:, c * 8 : (c + 1) * 8, :].reshape(HOLD * SLOT_B, LANE).astype(bf16)
        chunks.append(jnp.concatenate([first, last], axis=0))
    first = jnp.concatenate(tails[:4], axis=1).reshape(ROW_A, LANE).astype(bf16)
    last = tails[4].reshape(HOLD * SLOT_B, LANE).astype(bf16)
    chunks.append(jnp.concatenate([first, last], axis=0))
    return jnp.concatenate(chunks, axis=1)


def fold(values):
    tail = values[:, REST:]
    for shift in (64, 32, 16):
        tail = tail + pltpu.roll(tail, shift, 1)
    return tail


def once(tail):
    return jnp.where(iota(tail.shape, 1) < TAIL, tail, 0.0)


def spread_tail(values):
    tail = values[:, REST:]
    for shift in (16, 32, 64):
        tail = tail + pltpu.roll(tail, shift, 1)
    return jnp.concatenate([values[:, :REST], tail], axis=1)


def serve(chosen, left, right, out_ref):
    both = jnp.concatenate([left, right], axis=1)
    table = jnp.concatenate([both[:REST]] + [both[REST:]] * 8, axis=0).astype(bf16)
    pack(mm_nt(chosen, table), out_ref)


def serve_kernel(left_ref, right_ref, got_ref, out_ref):
    serve(asked(got_ref, 0).astype(bf16), left_ref[...], right_ref[...], out_ref)


def unit(vectors):
    length = jnp.sqrt(jnp.sum(vectors * vectors, axis=-1, keepdims=True) + tiny)
    return vectors / length, length


def unit_back(grad, direction, length):
    return (grad - direction * jnp.sum(direction * grad, axis=-1, keepdims=True)) / length


def grad_kernel(in_ref, to_edge_ref, to_slot_ref, scale_ref, out_ref):
    rows = unpack(in_ref)

    def picked(kind):
        values = mm(to_edge_ref[kind * K : (kind + 1) * K, :], rows)
        return jnp.concatenate([values[:, :REST], once(fold(values))], axis=1)

    scale = scale_ref[...]
    query, query_len = unit(picked(0) * scale)
    noise, noise_len = unit(picked(2))
    query_half = query.astype(bf16)
    noise_half = noise.astype(bf16)
    target, target_len = unit(picked(1))
    positive = sharp * jnp.sum(query * target, axis=1, keepdims=True)
    scores = sharp * mm_nt(query_half, noise_half)
    raised = jnp.exp(positive)
    spread = jnp.exp(scores)
    total = raised + jnp.sum(spread, axis=1, keepdims=True)
    miss = raised / total - 1.0
    weights = spread / total
    query_grad = sharp * (miss * target + mm(weights.astype(bf16), noise_half))
    target_grad = sharp * miss * query
    noise_grad = sharp * mm(jnp.transpose(weights).astype(bf16), query_half)
    grads = [
        unit_back(query_grad, query, query_len) * scale,
        unit_back(target_grad, target, target_len),
        unit_back(noise_grad, noise, noise_len),
    ]
    together = jnp.concatenate([spread_tail(grad).astype(bf16) for grad in grads], axis=0)
    pack(mm(to_slot_ref[...], together), out_ref)


def adagrad(matrix, state, grad):
    state = state + jnp.sum(grad * grad, axis=0, keepdims=True) / D
    return matrix - rate * grad / (jnp.sqrt(state) + guard), state


def update(in_ref, to_row_ref, left_ref, right_ref, left_state_ref, right_state_ref):
    values = mm(to_row_ref[...], unpack(in_ref))
    values = jnp.concatenate([values[:, :REST], fold(values)], axis=1)
    turned = jnp.transpose(values)[:D]
    left, left_state = adagrad(left_ref[...], left_state_ref[...], turned[:, :K])
    right, right_state = adagrad(right_ref[...], right_state_ref[...], turned[:, K:])
    return left, left_state, right, right_state


def next_kernel(
    in_ref, to_row_ref, left_ref, right_ref, left_state_ref, right_state_ref, serve_ref,
    out_ref, left_out, left_state_out, right_out, right_state_out,
):
    left, left_state, right, right_state = update(
        in_ref, to_row_ref, left_ref, right_ref, left_state_ref, right_state_ref
    )
    left_out[...], left_state_out[...] = left, left_state
    right_out[...], right_state_out[...] = right, right_state
    serve(serve_ref[...], left, right, out_ref)


def last_kernel(
    in_ref, to_row_ref, left_ref, right_ref, left_state_ref, right_state_ref,
    left_out, left_state_out, right_out, right_state_out,
):
    left, left_state, right, right_state = update(
        in_ref, to_row_ref, left_ref, right_ref, left_state_ref, right_state_ref
    )
    left_out[...], left_state_out[...] = left, left_state
    right_out[...], right_state_out[...] = right, right_state


def call(kernel, outs, *args, flops=0):
    size = sum(x.size * x.dtype.itemsize for x in list(args) + list(outs))
    spec = pl.BlockSpec(memory_space=pltpu.VMEM)
    return pl.pallas_call(
        kernel,
        out_shape=tuple(outs),
        in_specs=[spec] * len(args),
        out_specs=tuple([spec] * len(outs)),
        compiler_params=pltpu.CompilerParams(vmem_limit_bytes=40 * 1024 * 1024),
        cost_estimate=pl.CostEstimate(flops=flops, bytes_accessed=size, transcendentals=0),
    )(*args)


def shape(dims, dtype):
    return jax.ShapeDtypeStruct(dims, dtype)


def exchange(blocks):
    return lax.all_to_all(blocks, "edge", split_axis=0, concat_axis=0, tiled=True)


def shifted(value, axis, steps):
    count = lax.axis_size(axis)
    pairs = [(source, (source + steps) % count) for source in range(count)]
    return lax.ppermute(value, axis, pairs)


BLOCKS = shape((HOLD, BLOCK, LANE), bf16)
TABLE = shape((D, K), f32)
STATE = shape((1, K), f32)


def on_device(
    left_emb, right_emb, left_state, right_state, relations, src_rows, dst_rows, rel_ids, neg_rows
):
    left, right = left_emb.T, right_emb.T
    left_hist, right_hist = left_state.reshape(1, K), right_state.reshape(1, K)
    want, place = call(
        plan_kernel,
        [shape((HOLD, 1, LANE), i32), shape((8, K), i32)],
        src_rows[0], dst_rows[0], neg_rows[0],
    )
    got = exchange(want)
    to_slot_0, to_edge_0, to_slot_1, to_edge_1 = call(
        edge_kernel,
        [shape((ROWS_J, 3 * K), bf16), shape((3 * K, ROWS_J), bf16)] * 2,
        place,
    )
    scales = jnp.pad(relations[rel_ids[0].reshape(-1)], ((0, 0), (0, WIDE - D)))
    (blocks,) = call(serve_kernel, [BLOCKS], left, right, got)
    blocks = exchange(blocks)
    sum_first, serve_second, sum_second = call(
        held_kernel,
        [
            shape((2 * K, ROWS_J), bf16),
            shape((ROWS_J, 2 * K), bf16),
            shape((2 * K, ROWS_J), bf16),
        ],
        got,
    )
    (blocks,) = call(grad_kernel, [BLOCKS], blocks, to_edge_0, to_slot_0, scales[:K])
    blocks = exchange(blocks)
    blocks, left, left_hist, right, right_hist = call(
        next_kernel,
        [BLOCKS, TABLE, STATE, TABLE, STATE],
        blocks, sum_first, left, right, left_hist, right_hist, serve_second,
    )
    blocks = exchange(blocks)
    (blocks,) = call(grad_kernel, [BLOCKS], blocks, to_edge_1, to_slot_1, scales[K:])
    blocks = exchange(blocks)
    left, left_hist, right, right_hist = call(
        last_kernel,
        [TABLE, STATE, TABLE, STATE],
        blocks, sum_second, left, right, left_hist, right_hist,
    )
    right, right_hist = shifted((right, right_hist), "bucket", 1)
    return (left.T, left_hist.reshape(K), right.T, right_hist.reshape(K))


def solution(mesh):
    return jax.shard_map(
        on_device,
        mesh=mesh,
        in_specs=(
            P(("bucket", "edge"), None),
            P(("bucket", "edge"), None),
            P(("bucket", "edge")),
            P(("bucket", "edge")),
            P(),
            P("bucket", None, "edge"),
            P("bucket", None, "edge"),
            P("bucket", None, "edge"),
            P("bucket", None, "edge"),
        ),
        out_specs=(
            P(("bucket", "edge"), None),
            P(("bucket", "edge")),
            P(("bucket", "edge"), None),
            P(("bucket", "edge")),
        ),
        check_vma=False,
    )
```

profile of v0, /device:TPU:8, one launch (start us, length us, event | category | flops | bytes accessed | tf_op | source)
XLA Modules:
  0.0 201.3 jit_solution(1818548814175545748)
XLA Ops:
  3.2 27.0 %all_to_all.25.got_ref = s32[32,1,128]{2,1,0:T(1,128)S(1)} all-to-all(s32[32,1,128]{2,1,0:T(1,128)S(1)} %get-tuple-element.22), channel_id=1, replica_groups=mesh['bucket'=16,'edge'=32] {'edge'}, dimensions={0} | all-to-all | bytes 32768 | tf_op jit(solution)/shard_map/all_to_all | solution.py:282
  32.2 1.9 shard_map.121
  34.1 5.0 %all-to-all-start.1 = ((bf16[32,120,128]{2,1,0:T(8,128)(2,1)}), bf16[32,120,128]{2,1,0:T(8,128)(2,1)S(1)}, u32[]{:S(2)}, u32[]{:S(2)}) async-start(bf16[32,120,128]{2,1,0:T(8,128)(2,1)} %shard_map.121), calls=%async_computation.1 | async-start | bytes 1966080 | tf_op jit(solution)/shard_map/all_to_all | solution.py:282
  39.1 2.5 %shard_map.122 = (bf16[1280,768]{1,0:T(8,128)(2,1)S(1)}, bf16[768,1280]{1,0:T(8,128)(2,1)S(1)}, bf16[1280,768]{1,0:T(8,128)(2,1)S(1)}, bf16[768,1280]{1,0:T(8,128)(2,1)S(1)}) custom-call(s32[8,256]{1,0:T(8,128)S(1)} %get-tuple-element.23.place_ref), custom_call_target="tpu_custom_call" | custom-call | bytes 7872512 | tf_op jit(solution)/shard_map/pallas_call | solution.py:267
  42.9 1.3 copy-done.2
  44.2 1.3 copy-done.4
  46.8 1.8 copy.13
  48.7 3.6 %gather_fusion = f32[512,400]{1,0:T(8,128)S(1)} fusion(f32[1024,400]{1,0:T(8,128)} %copy.13, s32[1024]{0:T(1024)S(1)} %pad_clamp_fusion), kind=kCustom, calls=%fused_computation | custom fusion | bytes 1640448 | tf_op jit(solution)/shard_map/gather | solution.py:312
  52.4 15.4 %all-to-all-done.1.in_ref = bf16[32,120,128]{2,1,0:T(8,128)(2,1)S(1)} async-done(((bf16[32,120,128]{2,1,0:T(8,128)(2,1)}), bf16[32,120,128]{2,1,0:T(8,128)(2,1)S(1)}, u32[]{:S(2)}, u32[]{:S(2)}) %all-to-all-start.1) | async-done | bytes 983072 | tf_op jit(solution)/shard_map/all_to_all | solution.py:282
  67.8 1.5 copy-done.5
  69.4 1.5 copy-done.7
  70.9 4.4 %shard_map.123 = bf16[32,120,128]{2,1,0:T(8,128)(2,1)} custom-call(bf16[32,120,128]{2,1,0:T(8,128)(2,1)S(1)} %all-to-all-done.1.in_ref, bf16[768,1280]{1,0:T(8,128)(2,1)S(1)} %copy-done.7, bf16[1280,768]{1,0:T(8,128)(2,1)S(1)} %copy-done.5, f32[256,512]{1,0:T(8,128)S(1)} %get-tuple-element.41.scale_ref), custom_call_target="tpu_custom_call" | custom-call | bytes 6422528 | tf_op jit(solution)/shard_map/pallas_call | solution.py:267
  75.4 5.7 %all-to-all-start.2 = ((bf16[32,120,128]{2,1,0:T(8,128)(2,1)}), bf16[32,120,128]{2,1,0:T(8,128)(2,1)S(1)}, u32[]{:S(2)}, u32[]{:S(2)}) async-start(bf16[32,120,128]{2,1,0:T(8,128)(2,1)} %shard_map.123), calls=%async_computation.2 | async-start | bytes 1966080 | tf_op jit(solution)/shard_map/all_to_all | solution.py:282
  81.1 1.7 shard_map.124
  86.1 23.6 %all-to-all-done.2.in_ref = bf16[32,120,128]{2,1,0:T(8,128)(2,1)S(1)} async-done(((bf16[32,120,128]{2,1,0:T(8,128)(2,1)}), bf16[32,120,128]{2,1,0:T(8,128)(2,1)S(1)}, u32[]{:S(2)}, u32[]{:S(2)}) %all-to-all-start.2) | async-done | bytes 983072 | tf_op jit(solution)/shard_map/all_to_all | solution.py:282
  111.1 1.3 copy-done.17
  112.4 2.3 %shard_map.125 = (bf16[32,120,128]{2,1,0:T(8,128)(2,1)S(1)}, f32[400,256]{1,0:T(8,128)S(1)}, f32[1,256]{1,0:T(1,128)S(1)}, f32[400,256]{1,0:T(8,128)S(1)}, f32[1,256]{1,0:T(1,128)S(1)}) custom-call(bf16[32,120,128]{2,1,0:T(8,128)(2,1)S(1)} %all-to-all-done.2.in_ref, bf16[512,1280]{1,0:T(8,128)(2,1)S(1)} %copy-done.15, f32[400,256]{1,0:T(8,128)S(1)} %bitcast.16, ...), custom_call_target="tpu_custom_call" | custom-call | bytes 6230016 | tf_op jit(solution)/shard_map/pallas_call | solution.py:267
  114.6 34.1 %all_to_all.26.in_ref = bf16[32,120,128]{2,1,0:T(8,128)(2,1)S(1)} all-to-all(bf16[32,120,128]{2,1,0:T(8,128)(2,1)S(1)} %get-tuple-element.28), channel_id=1, replica_groups=mesh['bucket'=16,'edge'=32] {'edge'}, dimensions={0} | all-to-all | bytes 1966080 | tf_op jit(solution)/shard_map/all_to_all | solution.py:282
  148.7 3.6 %shard_map.126 = bf16[32,120,128]{2,1,0:T(8,128)(2,1)S(1)} custom-call(bf16[32,120,128]{2,1,0:T(8,128)(2,1)S(1)} %all_to_all.26.in_ref, bf16[768,1280]{1,0:T(8,128)(2,1)S(1)} %copy-done.3, bf16[1280,768]{1,0:T(8,128)(2,1)S(1)} %copy-done.1, f32[256,512]{1,0:T(8,128)S(1)} %get-tuple-element.40.scale_ref), custom_call_target="tpu_custom_call" | custom-call | bytes 6422528 | tf_op jit(solution)/shard_map/pallas_call | solution.py:267
  152.3 33.9 %all_to_all.27.in_ref = bf16[32,120,128]{2,1,0:T(8,128)(2,1)S(1)} all-to-all(bf16[32,120,128]{2,1,0:T(8,128)(2,1)S(1)} %shard_map.126), channel_id=1, replica_groups=mesh['bucket'=16,'edge'=32] {'edge'}, dimensions={0} | all-to-all | bytes 1966080 | tf_op jit(solution)/shard_map/all_to_all | solution.py:282
  186.2 2.4 %shard_map.127 = (f32[400,256]{1,0:T(8,128)}, f32[1,256]{1,0:T(1,128)}, f32[400,256]{1,0:T(8,128)S(1)}, f32[1,256]{1,0:T(1,128)S(1)}) custom-call(bf16[32,120,128]{2,1,0:T(8,128)(2,1)S(1)} %all_to_all.27.in_ref, bf16[512,1280]{1,0:T(8,128)(2,1)S(1)} %copy-done.13, f32[400,256]{1,0:T(8,128)S(1)} %get-tuple-element.32.left_ref, ...), custom_call_target="tpu_custom_call" | custom-call | bytes 3936256 | tf_op jit(solution)/shard_map/pallas_call | solution.py:267
  188.6 1.9 collective-permute-start
  190.5 3.7 %collective-permute-start.1 = (f32[1,256]{1,0:T(1,128)S(1)}, f32[1,256]{1,0:T(1,128)S(1)}, u32[]{:S(2)}, u32[]{:S(2)}) collective-permute-start(f32[1,256]{1,0:T(1,128)S(1)} %get-tuple-element.39), channel_id=1, source_target_pairs={{0,32},{32,64},{64,96},{96,128},{128,160},{160,192},{192,224},{224... | collective-permute-start | bytes 3080 | tf_op jit(solution)/shard_map/ppermute | solution.py:288
  194.2 5.8 %collective-permute-done.1 = f32[1,256]{1,0:T(1,128)S(1)} collective-permute-done((f32[1,256]{1,0:T(1,128)S(1)}, f32[1,256]{1,0:T(1,128)S(1)}, u32[]{:S(2)}, u32[]{:S(2)}) %collective-permute-start.1) | collective-permute-done | bytes 1056 | tf_op jit(solution)/shard_map/ppermute | solution.py:288
  (53 shorter events, 13.1 us)
Async XLA Ops:
  32.1 14.7 %copy-start.23 = (f32[1024,400]{0,1:T(8,128)S(1)}, f32[1024,400]{0,1:T(8,128)}, u32[]{:S(2)}) copy-start(f32[1024,400]{0,1:T(8,128)} %param.13) | copy-start | bytes 4915204
  34.1 33.7 %all-to-all-start.1 = ((bf16[32,120,128]{2,1,0:T(8,128)(2,1)}), bf16[32,120,128]{2,1,0:T(8,128)(2,1)S(1)}, u32[]{:S(2)}, u32[]{:S(2)}) async-start(bf16[32,120,128]{2,1,0:T(8,128)(2,1)} %shard_map.121), calls=%async_computation.1 | async-start | bytes 1966080 | tf_op jit(solution)/shard_map/all_to_all | solution.py:282
  39.1 9.6 %copy-start.24 = (s32[1,2,256]{2,1,0:T(2,128)S(1)}, s32[1,2,256]{2,1,0:T(2,128)}, u32[]{:S(2)}) copy-start(s32[1,2,256]{2,1,0:T(2,128)} %param.16) | copy-start | bytes 6148
  41.6 1.3 copy-start
  42.9 1.3 copy-start.2
  44.2 1.3 copy-start.4
  45.5 1.3 copy-start.6
  67.8 1.5 copy-start.5
  69.4 1.5 copy-start.7
  75.4 34.4 %copy-start.9 = (f32[256,400]{0,1:T(8,128)S(1)}, f32[256,400]{0,1:T(8,128)}, u32[]{:S(2)}) copy-start(f32[256,400]{0,1:T(8,128)} %param.9) | copy-start | bytes 1228804
  75.4 34.4 %copy-start.11 = (f32[256,400]{0,1:T(8,128)S(1)}, f32[256,400]{0,1:T(8,128)}, u32[]{:S(2)}) copy-start(f32[256,400]{0,1:T(8,128)} %param.10) | copy-start | bytes 1228804
  75.4 34.4 %copy-start.21 = (f32[256]{0:T(256)S(1)}, f32[256]{0:T(256)}, u32[]{:S(2)}) copy-start(f32[256]{0:T(256)} %param.11) | copy-start | bytes 3076
  75.4 34.4 %copy-start.22 = (f32[256]{0:T(256)S(1)}, f32[256]{0:T(256)}, u32[]{:S(2)}) copy-start(f32[256]{0:T(256)} %param.12) | copy-start | bytes 3076
  75.4 34.3 %all-to-all-start.2 = ((bf16[32,120,128]{2,1,0:T(8,128)(2,1)}), bf16[32,120,128]{2,1,0:T(8,128)(2,1)S(1)}, u32[]{:S(2)}, u32[]{:S(2)}) async-start(bf16[32,120,128]{2,1,0:T(8,128)(2,1)} %shard_map.123), calls=%async_computation.2 | async-start | bytes 1966080 | tf_op jit(solution)/shard_map/all_to_all | solution.py:282
  82.8 1.1 copy-start.12
  83.9 1.0 copy-start.14
  84.9 1.2 copy-start.16
  109.7 1.3 copy-start.15
  111.0 1.3 copy-start.17
  112.4 36.3 %copy-start.3 = (bf16[768,1280]{1,0:T(8,128)(2,1)S(1)}, bf16[768,1280]{1,0:T(8,128)(2,1)}, u32[]{:S(2)}) copy-start(bf16[768,1280]{1,0:T(8,128)(2,1)} %copy-done.2) | copy-start | bytes 5898244
  114.6 34.1 %copy-start.1 = (bf16[1280,768]{1,0:T(8,128)(2,1)S(1)}, bf16[1280,768]{1,0:T(8,128)(2,1)}, u32[]{:S(2)}) copy-start(bf16[1280,768]{1,0:T(8,128)(2,1)} %copy-done) | copy-start | bytes 5898244
  152.3 34.0 %copy-start.13 = (bf16[512,1280]{1,0:T(8,128)(2,1)S(1)}, bf16[512,1280]{1,0:T(8,128)(2,1)}, u32[]{:S(2)}) copy-start(bf16[512,1280]{1,0:T(8,128)(2,1)} %copy-done.12) | copy-start | bytes 3932164
  188.6 11.4 %collective-permute-start = (f32[400,256]{1,0:T(8,128)S(1)}, f32[400,256]{1,0:T(8,128)S(1)}, u32[]{:S(2)}, u32[]{:S(2)}) collective-permute-start(f32[400,256]{1,0:T(8,128)S(1)} %get-tuple-element.38), channel_id=1, source_target_pairs={{0,32},{32,64},{64,96},{96,128},{128,160},{160,192},{192,224},{224... | collective-permute-start | bytes 1228808 | tf_op jit(solution)/shard_map/ppermute | solution.py:288
  190.5 9.5 %collective-permute-start.1 = (f32[1,256]{1,0:T(1,128)S(1)}, f32[1,256]{1,0:T(1,128)S(1)}, u32[]{:S(2)}, u32[]{:S(2)}) collective-permute-start(f32[1,256]{1,0:T(1,128)S(1)} %get-tuple-element.39), channel_id=1, source_target_pairs={{0,32},{32,64},{64,96},{96,128},{128,160},{160,192},{192,224},{224... | collective-permute-start | bytes 3080 | tf_op jit(solution)/shard_map/ppermute | solution.py:288
  (5 other events, 4.0 us)
where the time goes:
time: 202 us; the launch traced here: 201 us
  blocking collectives  95 us (47%)
  waiting for transfers between devices  44.8 us (22%)
  local copies, waits for them, and re-layouts  25.1 us (12%)
  Pallas kernels  19.3 us (10%)
  starting transfers between devices  16.3 us (8%)
    all_to_all x3, blocking collectives, exchange(): lax.all_to_all(blocks, 'edge', split_axis=0, concat_axis=0, tiled=True)  95 us
    all_to_all x2, waiting for transfers between devices, exchange(): lax.all_to_all(blocks, 'edge', split_axis=0, concat_axis=0, tiled=True)  39 us
    unnamed x54, local copies, waits for them, and re-layouts  21.4 us
    pallas_call x8, Pallas kernels, call(): pl.pallas_call(kernel, out_shape=tuple(outs), in_specs=[spec] * len(args)...  19.3 us
    all_to_all x2, starting transfers between devices, exchange(): lax.all_to_all(blocks, 'edge', split_axis=0, concat_axis=0, tiled=True)  10.7 us
    ppermute x2, waiting for transfers between devices, shifted(): return lax.ppermute(value, axis, pairs)  5.77 us
    ppermute x2, starting transfers between devices, shifted(): return lax.ppermute(value, axis, pairs)  5.63 us
  transfers between devices with their start and end apart: 4, of which 3 were waited for; matrix products, arithmetic and copies ran while one was open for 3% of the time, Pallas kernels for 2%

commit v1 on v0

v1 whole, which is shorter than its diff:
```python
import functools

import jax
import jax.numpy as jnp
from jax import lax
from jax.experimental import pallas as pl
from jax.experimental.pallas import tpu as pltpu
from jax.sharding import PartitionSpec as P

SUBS = 2
D = 400
K = 256
HOLD = 32
CAP = 12
LANE = 128
WIDE = 512
TAIL = 16
REST = 3 * LANE
GROUP = 8
GROUPS = 5
PARTS = 6
GROUP_OF = (0, 1, 2, 3, 3, 4)
USED = 36
BLOCK = 3 * GROUPS * GROUP
MIB = 1024 * 1024
STEP = 64

sharp = 40.0
rate = 0.5
tiny = 1e-06
guard = 1e-10

f32 = jnp.float32
bf16 = jnp.bfloat16
i32 = jnp.int32


def iota(shape, dim):
    return lax.broadcasted_iota(i32, shape, dim)


def mm(first, second):
    return lax.dot_general(first, second, (((1,), (0,)), ((), ())), preferred_element_type=f32)


def mm_nt(first, second):
    return lax.dot_general(first, second, (((1,), (1,)), ((), ())), preferred_element_type=f32)


def as_half(mask):
    return mask.astype(f32).astype(bf16)


def load(pairs, sems):
    copies = [
        pltpu.make_async_copy(source, target, sems.at[number])
        for number, (source, target) in enumerate(pairs)
    ]
    for copy in copies:
        copy.start()
    return copies


def plan_kernel(src_far, dst_far, neg_far, want_ref, place_ref, src_ref, dst_ref, neg_ref, sems):
    refs = (src_ref, dst_ref, neg_ref)
    loads = load(zip((src_far, dst_far, neg_far), refs), sems)
    for copy in loads:
        copy.wait()
    lists = [refs[kind][step : step + 1, :] for step in range(SUBS) for kind in range(3)]
    holder = iota((HOLD, K), 0)
    hits = [(holder == (row >> 8)).astype(f32) for row in lists]
    upto = as_half(iota((K, K), 0) <= iota((K, K), 1))
    counts = mm(jnp.concatenate(hits, axis=0).astype(bf16), upto)
    want = jnp.zeros((HOLD, LANE), f32)
    slots = iota((LANE, K), 0)
    firsts, lasts = [], []
    for number, row in enumerate(lists):
        step, kind = divmod(number, 3)
        hit = hits[number]
        count = counts[number * HOLD : (number + 1) * HOLD, :]
        order = jnp.sum(hit * count, axis=0, keepdims=True).astype(i32) - 1
        early = order < GROUP
        late = order - GROUP + (4 if kind == 1 else 0)
        slot = jnp.where(early, kind * GROUP + order, GROUP_OF[3 + kind] * GROUP + late)
        owner = row >> 8
        local = (row & 255).astype(f32)
        chosen = as_half(slots == slot + step * STEP)
        want = want + mm_nt((hit * local).astype(bf16), chosen)
        firsts.append(jnp.where(early, owner * GROUP + order, -1))
        lasts.append(jnp.where(early, -1, owner * GROUP + late))
    places = firsts[:3] + lasts[:3] + firsts[3:] + lasts[3:] + [jnp.full((4, K), -1, i32)]
    place_ref[...] = jnp.concatenate(places, axis=0)
    slot = iota((HOLD, LANE), 1) & (STEP - 1)
    want_ref[:, 0, :] = want.astype(i32) + jnp.where(slot < USED, 0, 2 * K)


def part(number):
    return slice(number * K, (number + 1) * K)


def asked(got_ref, step):
    got = got_ref[:, 0, :].astype(f32)
    square = jnp.concatenate([got, jnp.zeros((LANE - HOLD, LANE), f32)], axis=0)
    turned = jnp.transpose(square).astype(i32)
    groups = []
    for group in range(GROUPS):
        start = step * STEP + group * GROUP
        rows = [
            (iota((GROUP, K), 1) == turned[start : start + GROUP, holder : holder + 1]).astype(f32)
            for holder in range(HOLD)
        ]
        groups.append(jnp.concatenate(rows, axis=0))
    half = (iota((K, K), 0) & (GROUP - 1)) < 4
    shared = groups[3]
    return groups[:3] + [jnp.where(half, shared, 0.0), jnp.where(half, 0.0, shared), groups[4]]


def held_kernel(step, got_ref, token_ref, sum_ref):
    del token_ref
    for number, rows in enumerate(asked(got_ref, step)):
        sum_ref[part(number), :] = jnp.transpose(rows).astype(bf16)


def group_mask(shape):
    return (iota(shape, len(shape) - 1) >> 4) == iota(shape, len(shape) - 2)


def pack(values, out_ref):
    keep = group_mask((HOLD, GROUP, LANE))
    sub = iota((HOLD, GROUP, LANE), 1)
    values = [value.reshape(HOLD, GROUP, WIDE) for value in values]
    pieces = [[value[:, :, c * LANE : (c + 1) * LANE] for value in values] for c in range(3)]
    for group, value in enumerate(values):
        row = jnp.sum(jnp.where(keep, value[:, :, REST:], 0.0), axis=1, keepdims=True)
        c, at = divmod(group, 4)
        pieces[c][4] = jnp.where(sub == 4 + at, row, pieces[c][4])
    out_ref[...] = jnp.concatenate(pieces[0] + pieces[1] + pieces[2], axis=1).astype(bf16)


def unpack(in_ref):
    keep = group_mask((HOLD, GROUP, LANE))
    rows = in_ref[...].astype(f32)
    groups = []
    for group in range(GROUPS):
        chunks = []
        for c in range(3):
            start = (c * GROUPS + group) * GROUP
            chunks.append(rows[:, start : start + GROUP, :])
        c, at = divmod(group, 4)
        start = (c * GROUPS + 4) * GROUP + 4 + at
        chunks.append(jnp.where(keep, rows[:, start : start + 1, :], 0.0))
        groups.append(
            jnp.concatenate([x.reshape(K, LANE) for x in chunks], axis=1).astype(bf16)
        )
    return groups


def fold(values):
    tail = values[:, REST:]
    for shift in (64, 32, 16):
        tail = tail + pltpu.roll(tail, shift, 1)
    return tail


def once(tail):
    return jnp.where(iota(tail.shape, 1) < TAIL, tail, 0.0)


def spread_tail(values):
    tail = values[:, REST:]
    for shift in (16, 32, 64):
        tail = tail + pltpu.roll(tail, shift, 1)
    return jnp.concatenate([values[:, :REST], tail], axis=1)


def table_of(values):
    return jnp.concatenate([values[:REST]] + [values[REST:]] * 8, axis=0).astype(bf16)


def table_kernel(left_ref, right_ref, place_ref, out_ref, column_ref):
    place = place_ref[...].astype(f32)
    tall = jnp.concatenate([place, jnp.zeros((LANE - 16, K), f32)], axis=0)
    column_ref[...] = jnp.transpose(tall).astype(i32)
    out_ref[:, :K] = table_of(left_ref[...])
    out_ref[:, K:] = table_of(right_ref[...])


def serve(parts, left, right, out_ref):
    tables = (left, right, right, left, right, right)
    values = [mm_nt(rows, table) for rows, table in zip(parts, tables)]
    pack(values[:3] + [values[3] + values[4], values[5]], out_ref)


def serve_kernel(table_ref, got_ref, out_ref, token_ref):
    token_ref[...] = jnp.zeros_like(token_ref)
    parts = [rows.astype(bf16) for rows in asked(got_ref, 0)]
    serve(parts, table_ref[:, :K], table_ref[:, K:], out_ref)


def unit(vectors):
    inverse = 1.0 / jnp.sqrt(jnp.sum(vectors * vectors, axis=-1, keepdims=True) + tiny)
    return vectors * inverse, inverse


def unit_back(grad, direction, inverse):
    return (grad - direction * jnp.sum(direction * grad, axis=-1, keepdims=True)) * inverse


def grad_kernel(step, in_ref, column_ref, place_ref, scale_ref, *refs):
    out_ref = refs[-1]
    rows = unpack(in_ref)

    def picked_part(number):
        at = step * PARTS + number
        to_edge = as_half(iota((K, K), 1) == column_ref[:, at : at + 1])
        return mm(to_edge, rows[GROUP_OF[number]])

    def picked(kind):
        values = picked_part(kind) + picked_part(3 + kind)
        return jnp.concatenate([values[:, :REST], once(fold(values))], axis=1)

    scale = scale_ref[...]
    query, query_inv = unit(picked(0) * scale)
    noise, noise_inv = unit(picked(2))
    query_half = query.astype(bf16)
    noise_half = noise.astype(bf16)
    target, target_inv = unit(picked(1))
    positive = sharp * jnp.sum(query * target, axis=1, keepdims=True)
    scores = sharp * mm_nt(query_half, noise_half)
    raised = jnp.exp(positive)
    spread = jnp.exp(scores)
    total = raised + jnp.sum(spread, axis=1, keepdims=True)
    share = 1.0 / total
    miss = raised * share - 1.0
    weights = spread * share
    query_grad = sharp * (miss * target + mm(weights.astype(bf16), noise_half))
    target_grad = sharp * miss * query
    noise_grad = sharp * mm(jnp.transpose(weights).astype(bf16), query_half)
    grads = [
        unit_back(query_grad, query, query_inv) * scale,
        unit_back(target_grad, target, target_inv),
        unit_back(noise_grad, noise, noise_inv),
    ]
    grads = [spread_tail(grad).astype(bf16) for grad in grads]
    values = []
    for number in range(PARTS):
        at = step * PARTS + number
        to_slot = as_half(iota((K, K), 0) == place_ref[at : at + 1, :])
        values.append(mm(to_slot, grads[number % 3]))
    pack(values[:3] + [values[3] + values[4], values[5]], out_ref)


def adagrad(matrix, state, grad):
    state = state + jnp.sum(grad * grad, axis=0, keepdims=True) / D
    return matrix - grad * (rate / (jnp.sqrt(state) + guard)), state


def row_grads(rows, to_row_ref, numbers):
    values = sum(mm(to_row_ref[part(number), :], rows[GROUP_OF[number]]) for number in numbers)
    values = jnp.concatenate([values[:, :REST], fold(values)], axis=1)
    return jnp.transpose(values)[:D]


LEFT = (0, 3)
RIGHT = (1, 2, 4, 5)


def update(in_ref, to_row_ref, left_ref, right_ref, left_state_ref, right_state_ref):
    rows = unpack(in_ref)
    left = adagrad(left_ref[...], left_state_ref[...], row_grads(rows, to_row_ref, LEFT))
    right = adagrad(right_ref[...], right_state_ref[...], row_grads(rows, to_row_ref, RIGHT))
    return left, right


def next_kernel(
    in_ref, to_row_ref, left_ref, right_ref, left_state_ref, right_state_ref, got_ref,
    out_ref, token_ref,
):
    left, right = update(
        in_ref, to_row_ref, left_ref, right_ref, left_state_ref, right_state_ref
    )
    token_ref[...] = left[0][:8, :LANE]
    parts = [rows.astype(bf16) for rows in asked(got_ref, 1)]
    serve(parts, table_of(left[0]), table_of(right[0]), out_ref)


def update_kernel(
    in_ref, to_row_ref, left_ref, right_ref, left_state_ref, right_state_ref, token_ref,
    left_out, left_state_out, right_out, right_state_out,
):
    del token_ref
    left, right = update(
        in_ref, to_row_ref, left_ref, right_ref, left_state_ref, right_state_ref
    )
    left_out[...], left_state_out[...] = left
    right_out[...], right_state_out[...] = right


def right_last_kernel(in_ref, to_row_ref, right_ref, right_state_ref, joined_ref):
    grads = row_grads(unpack(in_ref), to_row_ref, RIGHT)
    right, state = adagrad(right_ref[...], right_state_ref[...], grads)
    joined_ref[...] = jnp.concatenate([right, jnp.broadcast_to(state, (8, K))], axis=0)


def left_last_kernel(in_ref, to_row_ref, left_ref, left_state_ref, left_out, left_state_out):
    grads = row_grads(unpack(in_ref), to_row_ref, LEFT)
    left_out[...], left_state_out[...] = adagrad(left_ref[...], left_state_ref[...], grads)


def call(kernel, outs, *args, far=(), scratch=(), copies=0, grant=16):
    size = sum(x.size * x.dtype.itemsize for x in list(args) + list(outs))
    held = pl.BlockSpec(memory_space=pltpu.VMEM)
    away = pl.BlockSpec(memory_space=pltpu.HBM)
    scratch = [pltpu.VMEM(x.shape, x.dtype) for x in scratch]
    if copies:
        scratch.append(pltpu.SemaphoreType.DMA((copies,)))
    return pl.pallas_call(
        kernel,
        out_shape=tuple(outs),
        in_specs=[away if number in far else held for number in range(len(args))],
        out_specs=tuple([held] * len(outs)),
        scratch_shapes=scratch,
        compiler_params=pltpu.CompilerParams(vmem_limit_bytes=grant * MIB),
        cost_estimate=pl.CostEstimate(flops=0, bytes_accessed=size, transcendentals=0),
    )(*args)


def shape(dims, dtype):
    return jax.ShapeDtypeStruct(dims, dtype)


def exchange(blocks):
    return lax.all_to_all(blocks, "edge", split_axis=0, concat_axis=0, tiled=True)


def exchange_in_turn(want):
    even = lax.axis_index("bucket") % 2 == 0
    count = lax.axis_size("bucket")
    first = lax.cond(even, exchange, jnp.zeros_like, want)
    signal = lax.ppermute(first[0], "bucket", [(b, b + 1) for b in range(0, count - 1, 2)])
    want = jnp.where(signal[0, 0] < 0, 0, want)
    return lax.cond(even, lambda one, two: one, lambda one, two: exchange(two), first, want)


def shifted(value, axis, steps):
    count = lax.axis_size(axis)
    pairs = [(source, (source + steps) % count) for source in range(count)]
    return lax.ppermute(value, axis, pairs)


BLOCKS = shape((HOLD, BLOCK, LANE), bf16)
TABLE = shape((D, K), f32)
STATE = shape((1, K), f32)
LIST = shape((SUBS, K), i32)
HOT = shape((PARTS * K, K), bf16)
TOKEN = shape((8, LANE), f32)


def holds_of(step, got, token):
    return call(functools.partial(held_kernel, step), [HOT], got, token)[0]


def grads_of(step, blocks, columns, place, scales, *tokens):
    return call(
        functools.partial(grad_kernel, step), [BLOCKS],
        blocks, columns, place, scales[step * K : (step + 1) * K], *tokens,
    )[0]


def on_device(
    left_emb, right_emb, left_state, right_state, relations, src_rows, dst_rows, rel_ids, neg_rows
):
    left, right = left_emb.T, right_emb.T
    left_hist, right_hist = left_state.reshape(1, K), right_state.reshape(1, K)
    want, place = call(
        plan_kernel, [shape((HOLD, 1, LANE), i32), shape((16, K), i32)],
        src_rows[0], dst_rows[0], neg_rows[0],
        far=(0, 1, 2), scratch=(LIST, LIST, LIST), copies=3, grant=62,
    )
    got = exchange_in_turn(want)
    scales = jnp.pad(relations[rel_ids[0].reshape(-1)], ((0, 0), (0, WIDE - D)))
    table, columns = call(
        table_kernel, [shape((WIDE, 2 * K), bf16), shape((K, LANE), i32)], left, right, place
    )
    blocks, token = call(serve_kernel, [BLOCKS, TOKEN], table, got)
    blocks = exchange(blocks)
    to_row = holds_of(0, got, token)
    blocks = grads_of(0, blocks, columns, place, scales, to_row)
    blocks = exchange(blocks)
    held = (blocks, to_row, left, right, left_hist, right_hist)
    blocks, token = call(next_kernel, [BLOCKS, TOKEN], *held, got)
    blocks = exchange(blocks)
    left, left_hist, right, right_hist = call(
        update_kernel, [TABLE, STATE, TABLE, STATE], *held, token
    )
    to_row = holds_of(1, got, left_hist)
    blocks = grads_of(1, blocks, columns, place, scales, to_row)
    blocks = exchange(blocks)
    (joined,) = call(
        right_last_kernel, [shape((D + 8, K), f32)], blocks, to_row, right, right_hist
    )
    joined = shifted(joined, "bucket", 1)
    left, left_hist = call(left_last_kernel, [TABLE, STATE], blocks, to_row, left, left_hist)
    return (left.T, left_hist.reshape(K), joined[:D].T, joined[D])


def solution(mesh):
    return jax.shard_map(
        on_device,
        mesh=mesh,
        in_specs=(
            P(("bucket", "edge"), None),
            P(("bucket", "edge"), None),
            P(("bucket", "edge")),
            P(("bucket", "edge")),
            P(),
            P("bucket", None, "edge"),
            P("bucket", None, "edge"),
            P("bucket", None, "edge"),
            P("bucket", None, "edge"),
        ),
        out_specs=(
            P(("bucket", "edge"), None),
            P(("bucket", "edge")),
            P(("bucket", "edge"), None),
            P(("bucket", "edge")),
        ),
        check_vma=False,
    )
```

time: 202 us -> 192 us (0.950)
  local copies, waits for them, and re-layouts: 25.1 us -> 17.8 us
  blocking collectives: 95 us -> 90 us
  starting transfers between devices: 16.3 us -> 19.5 us
    unnamed x54 -> x34, local copies, waits for them, and re-layouts: 21.4 us -> 10.1 us
    all_to_all x2, starting transfers between devices: 10.7 us -> 16.3 us  [exchange(): lax.all_to_all(blocks, 'edge', split_axis=0, concat_axis=0, tiled=True)]
    all_to_all x3, blocking collectives: 95 us -> 90 us  [exchange(): lax.all_to_all(blocks, 'edge', split_axis=0, concat_axis=0, tiled=True)]
    ppermute x2 -> x1, starting transfers between devices: 5.63 us -> 1.92 us  [shifted(): return lax.ppermute(value, axis, pairs)]
    slice x1 -> x2, local copies, waits for them, and re-layouts: 0.07 us -> 2.66 us  [the longest x1 2.09 us: grads_of(): scales[step * K:(step + 1) * K]]
    ppermute x2 -> x1, waiting for transfers between devices: 5.77 us -> 7.95 us  [shifted(): return lax.ppermute(value, axis, pairs)]
    pallas_call x8 -> x11, Pallas kernels: 19.3 us -> 17.9 us  [call(): pl.pallas_call(kernel, out_shape=tuple(outs), in_specs=[away if number in...]
  transfers between devices with their start and end apart: 4 -> 4, of which waited for: 3 -> 3; matrix products, arithmetic and copies ran while one was open for 3% -> 5% of each run, Pallas kernels for 2% -> 2%
where the time goes in v1:
time: 192 us
  blocking collectives  90 us (47%)
  waiting for transfers between devices  45.4 us (24%)
  starting transfers between devices  19.5 us (10%)
  Pallas kernels  17.9 us (9%)
  local copies, waits for them, and re-layouts  17.8 us (9%)
    all_to_all x3, blocking collectives, exchange(): lax.all_to_all(blocks, 'edge', split_axis=0, concat_axis=0, tiled=True)  90 us
    all_to_all x2, waiting for transfers between devices, exchange(): lax.all_to_all(blocks, 'edge', split_axis=0, concat_axis=0, tiled=True)  37.5 us
    pallas_call x11, Pallas kernels, call(): pl.pallas_call(kernel, out_shape=tuple(outs), in_specs=[away if number in...  17.9 us
    all_to_all x2, starting transfers between devices, exchange(): lax.all_to_all(blocks, 'edge', split_axis=0, concat_axis=0, tiled=True)  16.3 us
    unnamed x34, local copies, waits for them, and re-layouts  10.1 us
    ppermute x1, waiting for transfers between devices, shifted(): return lax.ppermute(value, axis, pairs)  7.95 us
    gather x1, local copies, waits for them, and re-layouts, on_device(): scales = jnp.pad(relations[rel_ids[0].reshape(-1)], ((0, 0), (0, WIDE - D)))  4.31 us
  transfers between devices with their start and end apart: 4, of which 3 were waited for; matrix products, arithmetic and copies ran while one was open for 5% of the time, Pallas kernels for 2%

profile of v1, /device:TPU:8, one launch (start us, length us, event | category | flops | bytes accessed | tf_op | source)
XLA Modules:
  0.0 191.7 jit_solution(6490112544873520181)
XLA Ops:
  0.6 1.6 shard_map.120
  2.3 27.0 %conditional.2 = (s32[32,1,128]{2,1,0:T(1,128)S(1)}) conditional(s32[]{:T(128)} %convert_element_type.6, () %tuple.21, s32[32,1,128]{2,1,0:T(1,128)S(1)} %get-tuple-element.42), branch_computations={%region_0.1_spmd, %region_1.2_spmd} | conditional | bytes 32776 | solution.py:339
  2.3 27.0 %all_to_all.28 = s32[32,1,128]{2,1,0:T(1,128)S(1)} all-to-all(s32[32,1,128]{2,1,0:T(1,128)S(1)} %param.1), channel_id=1, replica_groups=mesh['bucket'=16,'edge'=32] {'edge'}, dimensions={0} | all-to-all | bytes 32768 | tf_op jit(solution)/shard_map/cond/branch_1_fun/all_to_all | solution.py:333
  29.3 1.3 collective-permute-start
  30.6 1.0 copy-done
  31.6 1.0 copy-done.2
  33.4 1.6 shard_map.122
  35.1 5.0 %all-to-all-start.2 = ((bf16[32,120,128]{2,1,0:T(8,128)(2,1)}), bf16[32,120,128]{2,1,0:T(8,128)(2,1)S(1)}, u32[]{:S(2)}, u32[]{:S(2)}) async-start(bf16[32,120,128]{2,1,0:T(8,128)(2,1)} %get-tuple-element.43), calls=%async_computation.2 | async-start | bytes 1966080 | tf_op jit(solution)/shard_map/all_to_all | solution.py:333
  40.1 2.8 %copy.13 = f32[1024,400]{1,0:T(8,128)} copy(f32[1024,400]{0,1:T(8,128)} %param.17) | data formatting | bytes 3276800 | tf_op args[4]
  42.9 4.3 %gather_fusion = f32[512,400]{1,0:T(8,128)} fusion(f32[1024,400]{1,0:T(8,128)} %copy.13, s32[1024]{0:T(1024)S(1)} %pad_clamp_fusion), kind=kCustom, calls=%fused_computation | custom fusion | bytes 1640448 | tf_op jit(solution)/shard_map/gather | solution.py:381
  47.2 2.1 %pad_slice_fusion = (f32[256,512]{1,0:T(8,128)}, f32[256,512]{1,0:T(8,128)S(1)}) fusion(f32[512,400]{1,0:T(8,128)} %gather_fusion), kind=kLoop, calls=%fused_computation.2 | loop fusion | bytes 1867776 | tf_op jit(solution)/shard_map/slice | solution.py:366
  50.0 12.1 %all-to-all-done.2.in_ref = bf16[32,120,128]{2,1,0:T(8,128)(2,1)S(1)} async-done(((bf16[32,120,128]{2,1,0:T(8,128)(2,1)}), bf16[32,120,128]{2,1,0:T(8,128)(2,1)S(1)}, u32[]{:S(2)}, u32[]{:S(2)}) %all-to-all-start.2) | async-done | bytes 983072 | tf_op jit(solution)/shard_map/all_to_all | solution.py:333
  62.1 3.8 %shard_map.124 = bf16[32,120,128]{2,1,0:T(8,128)(2,1)S(1)} custom-call(bf16[32,120,128]{2,1,0:T(8,128)(2,1)S(1)} %all-to-all-done.2.in_ref, s32[256,128]{1,0:T(8,128)S(1)} %get-tuple-element.44.column_ref, s32[16,256]{1,0:T(8,128)S(1)} %copy-done.12, f32[256,512]{1,0:T(8,128)S(1)} %get-tuple-element.55.scale_ref, ...), custom_call_target="tpu_custom_call" | custom-call | bytes 3424256 | tf_op jit(solution)/shard_map/pallas_call | solution.py:317
  65.9 28.8 %all_to_all.30.in_ref = bf16[32,120,128]{2,1,0:T(8,128)(2,1)S(1)} all-to-all(bf16[32,120,128]{2,1,0:T(8,128)(2,1)S(1)} %shard_map.124), channel_id=1, replica_groups=mesh['bucket'=16,'edge'=32] {'edge'}, dimensions={0} | all-to-all | bytes 1966080 | tf_op jit(solution)/shard_map/all_to_all | solution.py:333
  94.7 1.8 shard_map.125
  97.5 11.3 %all-to-all-start.4 = ((bf16[32,120,128]{2,1,0:T(8,128)(2,1)}), bf16[32,120,128]{2,1,0:T(8,128)(2,1)S(1)}, u32[]{:S(2)}, u32[]{:S(2)}) async-start(bf16[32,120,128]{2,1,0:T(8,128)(2,1)} %copy-done.6), calls=%async_computation.4 | async-start | bytes 1966080 | tf_op jit(solution)/shard_map/all_to_all | solution.py:333
  109.9 1.3 shard_map.126
  113.4 25.4 %all-to-all-done.4.in_ref = bf16[32,120,128]{2,1,0:T(8,128)(2,1)S(1)} async-done(((bf16[32,120,128]{2,1,0:T(8,128)(2,1)}), bf16[32,120,128]{2,1,0:T(8,128)(2,1)S(1)}, u32[]{:S(2)}, u32[]{:S(2)}) %all-to-all-start.4) | async-done | bytes 983072 | tf_op jit(solution)/shard_map/all_to_all | solution.py:333
  138.8 1.0 copy-done.5
  139.8 3.8 %shard_map.128 = bf16[32,120,128]{2,1,0:T(8,128)(2,1)S(1)} custom-call(bf16[32,120,128]{2,1,0:T(8,128)(2,1)S(1)} %all-to-all-done.4.in_ref, s32[256,128]{1,0:T(8,128)S(1)} %get-tuple-element.44.column_ref, s32[16,256]{1,0:T(8,128)S(1)} %copy-done.12, f32[256,512]{1,0:T(8,128)S(1)} %copy-done.5, bf16[1536,256]{1,0:T(8,128)(2,1)S(1)} %shard_map.127.refs_0_.to_row_ref), custom_call_target="tpu_custom_call" | custom-call | bytes 3424256 | tf_op jit(solution)/shard_map/pallas_call | solution.py:317
  143.6 34.3 %all_to_all.31.in_ref = bf16[32,120,128]{2,1,0:T(8,128)(2,1)S(1)} all-to-all(bf16[32,120,128]{2,1,0:T(8,128)(2,1)S(1)} %shard_map.128), channel_id=1, replica_groups=mesh['bucket'=16,'edge'=32] {'edge'}, dimensions={0} | all-to-all | bytes 1966080 | tf_op jit(solution)/shard_map/all_to_all | solution.py:333
  178.9 1.9 %collective-permute-start.1 = (f32[408,256]{1,0:T(8,128)S(1)}, f32[408,256]{1,0:T(8,128)S(1)}, u32[]{:S(2)}, u32[]{:S(2)}) collective-permute-start(f32[408,256]{1,0:T(8,128)S(1)} %shard_map.130), channel_id=1, source_target_pairs={{0,32},{32,64},{64,96},{96,128},{128,160},{160,192},{192,224},{224... | collective-permute-start | bytes 1253384 | tf_op jit(solution)/shard_map/ppermute | solution.py:348
  180.8 1.6 shard_map.129
  182.4 7.9 %collective-permute-done.1 = f32[408,256]{1,0:T(8,128)S(1)} collective-permute-done((f32[408,256]{1,0:T(8,128)S(1)}, f32[408,256]{1,0:T(8,128)S(1)}, u32[]{:S(2)}, u32[]{:S(2)}) %collective-permute-start.1) | collective-permute-done | bytes 417824 | tf_op jit(solution)/shard_map/ppermute | solution.py:348
  (41 shorter events, 8.0 us)
Async XLA Ops:
  29.3 4.1 %collective-permute-start = (s32[1,128]{1,0:T(1,128)S(1)}, s32[1,128]{1,0:T(1,128)S(1)}, u32[]{:S(2)}, u32[]{:S(2)}) collective-permute-start(s32[1,128]{1,0:T(1,128)S(1)} %slice_bitcast_fusion.1), channel_id=1, source_target_pairs={{0,32},{64,96},{128,160},{192,224},{256,288},{320,352},{384,416},{... | collective-permute-start | bytes 1544 | tf_op jit(solution)/shard_map/ppermute | solution.py:340
  30.6 1.0 copy-start
  31.6 1.0 copy-start.2
  32.6 0.7 copy-start.11
  35.1 27.0 %all-to-all-start.2 = ((bf16[32,120,128]{2,1,0:T(8,128)(2,1)}), bf16[32,120,128]{2,1,0:T(8,128)(2,1)S(1)}, u32[]{:S(2)}, u32[]{:S(2)}) async-start(bf16[32,120,128]{2,1,0:T(8,128)(2,1)} %get-tuple-element.43), calls=%async_computation.2 | async-start | bytes 1966080 | tf_op jit(solution)/shard_map/all_to_all | solution.py:333
  40.0 2.9 %copy-start.15 = (s32[1,2,256]{2,1,0:T(2,128)S(1)}, s32[1,2,256]{2,1,0:T(2,128)}, u32[]{:S(2)}) copy-start(s32[1,2,256]{2,1,0:T(2,128)} %param.20) | copy-start | bytes 6148
  47.2 14.9 %copy-start.12 = (s32[16,256]{1,0:T(8,128)S(1)}, s32[16,256]{1,0:T(8,128)}, u32[]{:S(2)}) copy-start(s32[16,256]{1,0:T(8,128)} %get-tuple-element.40.place_ref) | copy-start | bytes 49156
  62.1 32.6 %copy-start.1 = (f32[256,400]{0,1:T(8,128)S(1)}, f32[256,400]{0,1:T(8,128)}, u32[]{:S(2)}) copy-start(f32[256,400]{0,1:T(8,128)} %param.13) | copy-start | bytes 1228804
  62.1 32.6 %copy-start.3 = (f32[256,400]{0,1:T(8,128)S(1)}, f32[256,400]{0,1:T(8,128)}, u32[]{:S(2)}) copy-start(f32[256,400]{0,1:T(8,128)} %param.14) | copy-start | bytes 1228804
  62.1 32.6 %copy-start.13 = (f32[256]{0:T(256)S(1)}, f32[256]{0:T(256)}, u32[]{:S(2)}) copy-start(f32[256]{0:T(256)} %param.15) | copy-start | bytes 3076
  62.1 32.6 %copy-start.14 = (f32[256]{0:T(256)S(1)}, f32[256]{0:T(256)}, u32[]{:S(2)}) copy-start(f32[256]{0:T(256)} %param.16) | copy-start | bytes 3076
  96.5 1.0 copy-start.6
  97.5 41.3 %all-to-all-start.4 = ((bf16[32,120,128]{2,1,0:T(8,128)(2,1)}), bf16[32,120,128]{2,1,0:T(8,128)(2,1)S(1)}, u32[]{:S(2)}, u32[]{:S(2)}) async-start(bf16[32,120,128]{2,1,0:T(8,128)(2,1)} %copy-done.6), calls=%async_computation.4 | async-start | bytes 1966080 | tf_op jit(solution)/shard_map/all_to_all | solution.py:333
  108.8 1.0 copy-start.4
  111.2 0.8 copy-start.7
  112.0 0.8 copy-start.9
  138.8 1.0 copy-start.5
  139.8 38.1 %copy-start.8 = (f32[400,256]{1,0:T(8,128)S(1)}, f32[400,256]{1,0:T(8,128)}, u32[]{:S(2)}) copy-start(f32[400,256]{1,0:T(8,128)} %copy-done.7) | copy-start | bytes 1228804
  143.6 37.2 %copy-start.10 = (f32[400,256]{1,0:T(8,128)S(1)}, f32[400,256]{1,0:T(8,128)}, u32[]{:S(2)}) copy-start(f32[400,256]{1,0:T(8,128)} %copy-done.9) | copy-start | bytes 1228804
  178.9 11.5 %collective-permute-start.1 = (f32[408,256]{1,0:T(8,128)S(1)}, f32[408,256]{1,0:T(8,128)S(1)}, u32[]{:S(2)}, u32[]{:S(2)}) collective-permute-start(f32[408,256]{1,0:T(8,128)S(1)} %shard_map.130), channel_id=1, source_target_pairs={{0,32},{32,64},{64,96},{96,128},{128,160},{160,192},{192,224},{224... | collective-permute-start | bytes 1253384 | tf_op jit(solution)/shard_map/ppermute | solution.py:348

commit v2 on v1

--- a/solution.py
+++ b/solution.py
@@ -177,7 +177,8 @@
     return jnp.concatenate([values[:REST]] + [values[REST:]] * 8, axis=0).astype(bf16)
 
 
-def table_kernel(left_ref, right_ref, place_ref, out_ref, column_ref):
+def table_kernel(left_ref, right_ref, place_ref, got_ref, out_ref, column_ref, signal_ref):
+    signal_ref[...] = got_ref[0]
     place = place_ref[...].astype(f32)
     tall = jnp.concatenate([place, jnp.zeros((LANE - 16, K), f32)], axis=0)
     column_ref[...] = jnp.transpose(tall).astype(i32)
@@ -333,15 +334,6 @@
     return lax.all_to_all(blocks, "edge", split_axis=0, concat_axis=0, tiled=True)
 
 
-def exchange_in_turn(want):
-    even = lax.axis_index("bucket") % 2 == 0
-    count = lax.axis_size("bucket")
-    first = lax.cond(even, exchange, jnp.zeros_like, want)
-    signal = lax.ppermute(first[0], "bucket", [(b, b + 1) for b in range(0, count - 1, 2)])
-    want = jnp.where(signal[0, 0] < 0, 0, want)
-    return lax.cond(even, lambda one, two: one, lambda one, two: exchange(two), first, want)
-
-
 def shifted(value, axis, steps):
     count = lax.axis_size(axis)
     pairs = [(source, (source + steps) % count) for source in range(count)]
@@ -377,11 +369,18 @@
         src_rows[0], dst_rows[0], neg_rows[0],
         far=(0, 1, 2), scratch=(LIST, LIST, LIST), copies=3, grant=62,
     )
-    got = exchange_in_turn(want)
+    even = lax.axis_index("bucket") % 2 == 0
+    first = lax.cond(even, exchange, jnp.zeros_like, want)
+    table, columns, signal = call(
+        table_kernel,
+        [shape((WIDE, 2 * K), bf16), shape((K, LANE), i32), shape((1, LANE), i32)],
+        left, right, place, first,
+    )
+    pairs = [(bucket, bucket + 1) for bucket in range(0, lax.axis_size("bucket") - 1, 2)]
+    signal = lax.ppermute(signal, "bucket", pairs)
+    want = jnp.where(signal[0, 0] < 0, 0, want)
+    got = lax.cond(even, lambda one, two: one, lambda one, two: exchange(two), first, want)
     scales = jnp.pad(relations[rel_ids[0].reshape(-1)], ((0, 0), (0, WIDE - D)))
-    table, columns = call(
-        table_kernel, [shape((WIDE, 2 * K), bf16), shape((K, LANE), i32)], left, right, place
-    )
     blocks, token = call(serve_kernel, [BLOCKS, TOKEN], table, got)
     blocks = exchange(blocks)
     to_row = holds_of(0, got, token)

time: 192 us -> 175 us (0.911)
  blocking collectives: 90 us -> 79.8 us
  waiting for transfers between devices: 45.4 us -> 37.1 us
    all_to_all x3, blocking collectives: 90 us -> 79.8 us  [exchange(): lax.all_to_all(blocks, 'edge', split_axis=0, concat_axis=0, tiled=True)]
    all_to_all x2, waiting for transfers between devices: 37.5 us -> 28.7 us  [exchange(): lax.all_to_all(blocks, 'edge', split_axis=0, concat_axis=0, tiled=True)]
    ppermute x1, starting transfers between devices: 1.92 us -> 10.3 us  [shifted(): return lax.ppermute(value, axis, pairs)]
    all_to_all x2, starting transfers between devices: 16.3 us -> 9.21 us  [exchange(): lax.all_to_all(blocks, 'edge', split_axis=0, concat_axis=0, tiled=True)]
  transfers between devices with their start and end apart: 4 -> 4, of which waited for: 3 -> 4; matrix products, arithmetic and copies ran while one was open for 5% -> 5% of each run, Pallas kernels for 2% -> 2%
where the time goes in v2:
time: 175 us; the launch traced here: 174 us
  blocking collectives  79.8 us (46%)
  waiting for transfers between devices  37.1 us (21%)
  starting transfers between devices  20.8 us (12%)
  Pallas kernels  17.9 us (10%)
  local copies, waits for them, and re-layouts  17.8 us (10%)
    all_to_all x3, blocking collectives, exchange(): lax.all_to_all(blocks, 'edge', split_axis=0, concat_axis=0, tiled=True)  79.8 us
    all_to_all x2, waiting for transfers between devices, exchange(): lax.all_to_all(blocks, 'edge', split_axis=0, concat_axis=0, tiled=True)  28.7 us
    pallas_call x11, Pallas kernels, call(): pl.pallas_call(kernel, out_shape=tuple(outs), in_specs=[away if number in...  17.9 us
    ppermute x1, starting transfers between devices, shifted(): return lax.ppermute(value, axis, pairs)  10.3 us
    unnamed x34, local copies, waits for them, and re-layouts  10.1 us
    all_to_all x2, starting transfers between devices, exchange(): lax.all_to_all(blocks, 'edge', split_axis=0, concat_axis=0, tiled=True)  9.21 us
    ppermute x1, waiting for transfers between devices, shifted(): return lax.ppermute(value, axis, pairs)  7.54 us
    gather x1, local copies, waits for them, and re-layouts, on_device(): scales = jnp.pad(relations[rel_ids[0].reshape(-1)], ((0, 0), (0, WIDE - D)))  4.31 us
  transfers between devices with their start and end apart: 4, of which 4 were waited for; matrix products, arithmetic and copies ran while one was open for 5% of the time, Pallas kernels for 2%

profile of v2, /device:TPU:8, one launch (start us, length us, event | category | flops | bytes accessed | tf_op | source)
XLA Modules:
  0.0 174.2 jit_solution(680249000511460979)
XLA Ops:
  0.6 1.6 shard_map.120
  2.3 27.0 %conditional.2 = (s32[32,1,128]{2,1,0:T(1,128)S(1)}) conditional(s32[]{:T(128)} %convert_element_type.6, () %tuple.21, s32[32,1,128]{2,1,0:T(1,128)S(1)} %get-tuple-element.42), branch_computations={%region_0.1_spmd, %region_1.2_spmd} | conditional | bytes 32776 | solution.py:373
  2.3 27.0 %all_to_all.28 = s32[32,1,128]{2,1,0:T(1,128)S(1)} all-to-all(s32[32,1,128]{2,1,0:T(1,128)S(1)} %param.1), channel_id=1, replica_groups=mesh['bucket'=16,'edge'=32] {'edge'}, dimensions={0} | all-to-all | bytes 32768 | tf_op jit(solution)/shard_map/cond/branch_1_fun/all_to_all | solution.py:334
  29.3 1.0 copy-done
  30.3 1.0 copy-done.2
  32.1 1.3 collective-permute-start
  34.2 1.6 shard_map.122
  35.8 5.0 %all-to-all-start.2 = ((bf16[32,120,128]{2,1,0:T(8,128)(2,1)}), bf16[32,120,128]{2,1,0:T(8,128)(2,1)S(1)}, u32[]{:S(2)}, u32[]{:S(2)}) async-start(bf16[32,120,128]{2,1,0:T(8,128)(2,1)} %get-tuple-element.45), calls=%async_computation.2 | async-start | bytes 1966080 | tf_op jit(solution)/shard_map/all_to_all | solution.py:334
  40.8 2.8 %copy.13 = f32[1024,400]{1,0:T(8,128)} copy(f32[1024,400]{0,1:T(8,128)} %param.17) | data formatting | bytes 3276800 | tf_op args[4]
  43.7 4.3 %gather_fusion = f32[512,400]{1,0:T(8,128)} fusion(f32[1024,400]{1,0:T(8,128)} %copy.13, s32[1024]{0:T(1024)S(1)} %pad_clamp_fusion), kind=kCustom, calls=%fused_computation | custom fusion | bytes 1640448 | tf_op jit(solution)/shard_map/gather | solution.py:383
  48.0 2.1 %pad_slice_fusion = (f32[256,512]{1,0:T(8,128)}, f32[256,512]{1,0:T(8,128)S(1)}) fusion(f32[512,400]{1,0:T(8,128)} %gather_fusion), kind=kLoop, calls=%fused_computation.2 | loop fusion | bytes 1867776 | tf_op jit(solution)/shard_map/slice | solution.py:358
  50.8 11.4 %all-to-all-done.2.in_ref = bf16[32,120,128]{2,1,0:T(8,128)(2,1)S(1)} async-done(((bf16[32,120,128]{2,1,0:T(8,128)(2,1)}), bf16[32,120,128]{2,1,0:T(8,128)(2,1)S(1)}, u32[]{:S(2)}, u32[]{:S(2)}) %all-to-all-start.2) | async-done | bytes 983072 | tf_op jit(solution)/shard_map/all_to_all | solution.py:334
  62.2 3.8 %shard_map.124 = bf16[32,120,128]{2,1,0:T(8,128)(2,1)S(1)} custom-call(bf16[32,120,128]{2,1,0:T(8,128)(2,1)S(1)} %all-to-all-done.2.in_ref, s32[256,128]{1,0:T(8,128)S(1)} %get-tuple-element.46.column_ref, s32[16,256]{1,0:T(8,128)S(1)} %copy-done.12, f32[256,512]{1,0:T(8,128)S(1)} %get-tuple-element.57.scale_ref, ...), custom_call_target="tpu_custom_call" | custom-call | bytes 3424256 | tf_op jit(solution)/shard_map/pallas_call | solution.py:318
  66.0 25.4 %all_to_all.30.in_ref = bf16[32,120,128]{2,1,0:T(8,128)(2,1)S(1)} all-to-all(bf16[32,120,128]{2,1,0:T(8,128)(2,1)S(1)} %shard_map.124), channel_id=1, replica_groups=mesh['bucket'=16,'edge'=32] {'edge'}, dimensions={0} | all-to-all | bytes 1966080 | tf_op jit(solution)/shard_map/all_to_all | solution.py:334
  91.4 1.8 %shard_map.125 = (bf16[32,120,128]{2,1,0:T(8,128)(2,1)S(1)}, f32[8,128]{1,0:T(8,128)S(1)}) custom-call(bf16[32,120,128]{2,1,0:T(8,128)(2,1)S(1)} %all_to_all.30.in_ref, bf16[1536,256]{1,0:T(8,128)(2,1)S(1)} %shard_map.123.refs_0_.to_row_ref, f32[400,256]{1,0:T(8,128)S(1)} %bitcast.19, f32[400,256]{1,0:T(8,128)S(1)} %bitcast.22, f32[1,256]{1,0:T(1,128)S(1)} %bitcast.24, ...), custom_call_target="tpu_custom_call" | custom-call | bytes 3594240 | tf_op jit(solution)/shard_map/pallas_call | solution.py:318
  94.2 4.2 %all-to-all-start.4 = ((bf16[32,120,128]{2,1,0:T(8,128)(2,1)}), bf16[32,120,128]{2,1,0:T(8,128)(2,1)S(1)}, u32[]{:S(2)}, u32[]{:S(2)}) async-start(bf16[32,120,128]{2,1,0:T(8,128)(2,1)} %copy-done.6), calls=%async_computation.4 | async-start | bytes 1966080 | tf_op jit(solution)/shard_map/all_to_all | solution.py:334
  99.4 1.3 shard_map.126
  103.0 17.3 %all-to-all-done.4.in_ref = bf16[32,120,128]{2,1,0:T(8,128)(2,1)S(1)} async-done(((bf16[32,120,128]{2,1,0:T(8,128)(2,1)}), bf16[32,120,128]{2,1,0:T(8,128)(2,1)S(1)}, u32[]{:S(2)}, u32[]{:S(2)}) %all-to-all-start.4) | async-done | bytes 983072 | tf_op jit(solution)/shard_map/all_to_all | solution.py:334
  120.3 1.0 copy-done.5
  121.3 3.8 %shard_map.128 = bf16[32,120,128]{2,1,0:T(8,128)(2,1)S(1)} custom-call(bf16[32,120,128]{2,1,0:T(8,128)(2,1)S(1)} %all-to-all-done.4.in_ref, s32[256,128]{1,0:T(8,128)S(1)} %get-tuple-element.46.column_ref, s32[16,256]{1,0:T(8,128)S(1)} %copy-done.12, f32[256,512]{1,0:T(8,128)S(1)} %copy-done.5, bf16[1536,256]{1,0:T(8,128)(2,1)S(1)} %shard_map.127.refs_0_.to_row_ref), custom_call_target="tpu_custom_call" | custom-call | bytes 3424256 | tf_op jit(solution)/shard_map/pallas_call | solution.py:318
  125.1 27.4 %all_to_all.31.in_ref = bf16[32,120,128]{2,1,0:T(8,128)(2,1)S(1)} all-to-all(bf16[32,120,128]{2,1,0:T(8,128)(2,1)S(1)} %shard_map.128), channel_id=1, replica_groups=mesh['bucket'=16,'edge'=32] {'edge'}, dimensions={0} | all-to-all | bytes 1966080 | tf_op jit(solution)/shard_map/all_to_all | solution.py:334
  153.5 10.3 %collective-permute-start.1 = (f32[408,256]{1,0:T(8,128)S(1)}, f32[408,256]{1,0:T(8,128)S(1)}, u32[]{:S(2)}, u32[]{:S(2)}) collective-permute-start(f32[408,256]{1,0:T(8,128)S(1)} %shard_map.130), channel_id=1, source_target_pairs={{0,32},{32,64},{64,96},{96,128},{128,160},{160,192},{192,224},{224... | collective-permute-start | bytes 1253384 | tf_op jit(solution)/shard_map/ppermute | solution.py:340
  163.8 1.6 shard_map.129
  165.4 7.5 %collective-permute-done.1 = f32[408,256]{1,0:T(8,128)S(1)} collective-permute-done((f32[408,256]{1,0:T(8,128)S(1)}, f32[408,256]{1,0:T(8,128)S(1)}, u32[]{:S(2)}, u32[]{:S(2)}) %collective-permute-start.1) | collective-permute-done | bytes 417824 | tf_op jit(solution)/shard_map/ppermute | solution.py:340
  (40 shorter events, 8.8 us)
Async XLA Ops:
  29.3 1.0 copy-start
  30.3 1.0 copy-start.2
  31.3 0.7 copy-start.11
  32.1 2.1 %collective-permute-start = (s32[1,128]{1,0:T(1,128)S(1)}, s32[1,128]{1,0:T(1,128)S(1)}, u32[]{:S(2)}, u32[]{:S(2)}) collective-permute-start(s32[1,128]{1,0:T(1,128)S(1)} %get-tuple-element.44), channel_id=1, source_target_pairs={{0,32},{64,96},{128,160},{192,224},{256,288},{320,352},{384,416},{... | collective-permute-start | bytes 1544 | tf_op jit(solution)/shard_map/ppermute | solution.py:380
  35.8 26.4 %all-to-all-start.2 = ((bf16[32,120,128]{2,1,0:T(8,128)(2,1)}), bf16[32,120,128]{2,1,0:T(8,128)(2,1)S(1)}, u32[]{:S(2)}, u32[]{:S(2)}) async-start(bf16[32,120,128]{2,1,0:T(8,128)(2,1)} %get-tuple-element.45), calls=%async_computation.2 | async-start | bytes 1966080 | tf_op jit(solution)/shard_map/all_to_all | solution.py:334
  40.8 2.9 %copy-start.15 = (s32[1,2,256]{2,1,0:T(2,128)S(1)}, s32[1,2,256]{2,1,0:T(2,128)}, u32[]{:S(2)}) copy-start(s32[1,2,256]{2,1,0:T(2,128)} %param.20) | copy-start | bytes 6148
  48.0 14.2 %copy-start.12 = (s32[16,256]{1,0:T(8,128)S(1)}, s32[16,256]{1,0:T(8,128)}, u32[]{:S(2)}) copy-start(s32[16,256]{1,0:T(8,128)} %get-tuple-element.41.place_ref) | copy-start | bytes 49156
  62.2 29.2 %copy-start.1 = (f32[256,400]{0,1:T(8,128)S(1)}, f32[256,400]{0,1:T(8,128)}, u32[]{:S(2)}) copy-start(f32[256,400]{0,1:T(8,128)} %param.13) | copy-start | bytes 1228804
  62.2 29.2 %copy-start.3 = (f32[256,400]{0,1:T(8,128)S(1)}, f32[256,400]{0,1:T(8,128)}, u32[]{:S(2)}) copy-start(f32[256,400]{0,1:T(8,128)} %param.14) | copy-start | bytes 1228804
  62.2 29.2 %copy-start.13 = (f32[256]{0:T(256)S(1)}, f32[256]{0:T(256)}, u32[]{:S(2)}) copy-start(f32[256]{0:T(256)} %param.15) | copy-start | bytes 3076
  62.2 29.2 %copy-start.14 = (f32[256]{0:T(256)S(1)}, f32[256]{0:T(256)}, u32[]{:S(2)}) copy-start(f32[256]{0:T(256)} %param.16) | copy-start | bytes 3076
  93.2 1.0 copy-start.6
  94.2 26.1 %all-to-all-start.4 = ((bf16[32,120,128]{2,1,0:T(8,128)(2,1)}), bf16[32,120,128]{2,1,0:T(8,128)(2,1)S(1)}, u32[]{:S(2)}, u32[]{:S(2)}) async-start(bf16[32,120,128]{2,1,0:T(8,128)(2,1)} %copy-done.6), calls=%async_computation.4 | async-start | bytes 1966080 | tf_op jit(solution)/shard_map/all_to_all | solution.py:334
  98.4 1.0 copy-start.4
  100.8 0.8 copy-start.7
  101.5 0.8 copy-start.9
  120.3 1.0 copy-start.5
  121.3 31.2 %copy-start.8 = (f32[400,256]{1,0:T(8,128)S(1)}, f32[400,256]{1,0:T(8,128)}, u32[]{:S(2)}) copy-start(f32[400,256]{1,0:T(8,128)} %copy-done.7) | copy-start | bytes 1228804
  125.1 38.6 %copy-start.10 = (f32[400,256]{1,0:T(8,128)S(1)}, f32[400,256]{1,0:T(8,128)}, u32[]{:S(2)}) copy-start(f32[400,256]{1,0:T(8,128)} %copy-done.9) | copy-start | bytes 1228804
  153.5 19.4 %collective-permute-start.1 = (f32[408,256]{1,0:T(8,128)S(1)}, f32[408,256]{1,0:T(8,128)S(1)}, u32[]{:S(2)}, u32[]{:S(2)}) collective-permute-start(f32[408,256]{1,0:T(8,128)S(1)} %shard_map.130), channel_id=1, source_target_pairs={{0,32},{32,64},{64,96},{96,128},{128,160},{160,192},{192,224},{224... | collective-permute-start | bytes 1253384 | tf_op jit(solution)/shard_map/ppermute | solution.py:340
